TPU v7x, 512 devices: a whole 4x8x8 slice. The times are simulated.
512 devices in a mesh: section: 32 (over x, y), tensor: 16 (over z, core).
Axes of the slice: x: 4, y: 8, z: 8, core: 2. Of those that a mesh axis runs over, the one named last changes fastest.
Arguments:
- frozen: bfloat16 [32, 14336, 2048], P('section', 'tensor'), may hold values from -1 to 1, as said below
- adapter_a: bfloat16 [32, 8, 14336], P('section', None, 'tensor'), may hold values from -0.119628906 to 0.119628906
- adapter_b: bfloat16 [32, 16, 2048], P('section'), may hold values from -0.22460938 to 0.22460938
- magnitude: float32 [32, 2048], P('section'), may hold values from 0.5 to 2
- hidden_fwd: bfloat16 [32, 128, 14336], P('section', None, 'tensor'), may hold values from -6 to 6
- carried: bfloat16 [32, 256, 2048], P('section', 'tensor'), may hold values from -6 to 6
- embedded: bfloat16 [256, 4096], P('tensor'), may hold values from -6 to 6
- hidden_bwd: bfloat16 [32, 128, 14336], P('section', None, 'tensor'), may hold values from -6 to 6
- returned: bfloat16 [32, 256, 2048], P('section', 'tensor'), may hold values from -1.5 to 1.5
- head_grad: bfloat16 [256, 4096], P('tensor'), may hold values from -1.5 to 1.5
Outputs:
- section_out: bfloat16 [32, 256, 2048], P('section', 'tensor')
- grad_magnitude: float32 [32, 2048], P('section')
- grad_a: float32 [32, 8, 14336], P('section', None, 'tensor')
- grad_b: float32 [32, 16, 2048], P('section')
- hidden_grad: bfloat16 [32, 128, 14336], P('section', None, 'tensor')
Inputs may be any that keep to these rules, and one draw needn't show every extreme that they name: frozen projection weights.
All inputs are finite; a program needn't handle non-finite values.
Results may differ from a plain program's by a relative error of at most 0.0057.
Values may be sent and summed in bfloat16 or wider, within the bound.
A program may use at most 64 MiB of HBM per device.

v0:
```python
import jax
import jax.numpy as jnp
from jax import lax
from jax.sharding import PartitionSpec as P

epsilon = 1e-06


def swapped(array, axis, apart):
    return lax.ppermute(array, axis, [(i, i ^ 1 << apart) for i in range(lax.axis_size(axis))])


def from_behind(array, axis, by):
    count = lax.axis_size(axis)
    pairs = [(i, i + by) for i in range(count) if 0 <= i + by < count]
    return lax.ppermute(array, axis, pairs)


def column_norms(squares):
    return jnp.sqrt(lax.psum(squares, "tensor") + epsilon)


def forward_rows(term_fn, own_rows):
    return lax.psum_scatter(
        term_fn(jnp.int32(0), own_rows * lax.axis_size("tensor")),
        "tensor",
        scatter_dimension=0,
        tiled=True,
    )


def local(
    frozen,
    adapter_a,
    adapter_b,
    magnitude,
    hidden_fwd,
    carried,
    embedded,
    hidden_bwd,
    returned,
    head_grad,
):
    base_w = frozen[0]
    fac_half = adapter_a[0]
    fac_b = adapter_b[0]
    mag = magnitude[0]
    own_rows = carried.shape[1]
    slot_id = lax.axis_index("section")
    slot_count = lax.axis_size("section")
    half = slot_id % 2
    first_half = half == 0
    fwd_other, bwd_other, fac_other = swapped(
        (hidden_fwd[0], hidden_bwd[0], fac_half), "section", 0
    )

    def in_order(own, other):
        return jnp.concatenate(
            [jnp.where(first_half, own, other), jnp.where(first_half, other, own)], axis=0
        )

    hid_fwd = in_order(hidden_fwd[0], fwd_other)
    hid_bwd = in_order(hidden_bwd[0], bwd_other)
    fac_a = in_order(fac_half, fac_other)
    width = base_w.shape[1]
    arriving = from_behind(carried[0], "section", 2)
    embed_cols = lax.dynamic_slice_in_dim(embedded, half * width, width, 1)
    inflow = jnp.where(slot_id < 2, embed_cols, arriving)
    coming = from_behind(returned[0], "section", -2)
    head_cols = lax.dynamic_slice_in_dim(head_grad, half * width, width, 1)
    cotangent = jnp.where(slot_id >= slot_count - 2, head_cols, coming)
    merged = (
        base_w.astype(jnp.float32)
        + jnp.einsum("rf,rd->fd", fac_a, fac_b, preferred_element_type=jnp.float32)
    ).astype(jnp.bfloat16)
    merged_f = merged.astype(jnp.float32)
    squares = jnp.sum(merged_f * merged_f, axis=0)
    low_part = jnp.einsum("tf,rf->tr", hid_bwd, fac_a, preferred_element_type=jnp.float32)
    low = lax.psum(low_part, "tensor").astype(jnp.bfloat16)
    col_norms = column_norms(squares)
    col_scale = mag / col_norms

    def scaled_term(offset, amount):
        return jnp.dot(hid_fwd, merged, preferred_element_type=jnp.float32) * col_scale

    projected = forward_rows(scaled_term, own_rows)
    section_out = (inflow.astype(jnp.float32) + projected).astype(jnp.bfloat16)
    all_rows = hid_bwd.shape[0]
    mag_acc = jnp.zeros((width,), jnp.float32)
    scaled_cot = (
        lax.all_gather(cotangent, "tensor", axis=0, tiled=True).astype(jnp.float32) * col_scale
    ).astype(jnp.bfloat16)
    hid_part = jnp.einsum("td,fd->tf", scaled_cot, merged, preferred_element_type=jnp.float32)
    hid_acc = hid_part
    adapt_part = jnp.einsum("td,rd->tr", scaled_cot, fac_b, preferred_element_type=jnp.float32)
    adapt_acc = adapt_part
    grad_b_acc = jnp.einsum("tr,td->rd", low, scaled_cot, preferred_element_type=jnp.float32)
    hid_acc, adapt_acc, grad_b_acc, mag_acc = (hid_acc, adapt_acc, grad_b_acc, mag_acc)
    half_rows = all_rows // 2
    send_hid = lax.dynamic_slice_in_dim(hid_acc, (1 - half) * half_rows, half_rows, 0)
    got_hid, got_adapt = swapped((send_hid, adapt_acc), "section", 0)
    own_hid = lax.dynamic_slice_in_dim(hid_acc, half * half_rows, half_rows, 0)
    hidden_grad = (own_hid + got_hid).astype(jnp.bfloat16)
    adapter_cot = (adapt_acc + got_adapt).astype(jnp.bfloat16)
    rank_half = fac_half.shape[0]
    own_cot = lax.dynamic_slice_in_dim(adapter_cot, half * rank_half, rank_half, 1)
    grad_a = jnp.einsum("tr,tf->rf", own_cot, hid_bwd, preferred_element_type=jnp.float32)
    own_recomputed = lax.psum_scatter(
        jnp.dot(hid_bwd, merged, preferred_element_type=jnp.float32),
        "tensor",
        scatter_dimension=0,
        tiled=True,
    )
    mag_part = jnp.sum(cotangent.astype(jnp.float32) * own_recomputed, axis=0)
    grad_mag = lax.psum(mag_part, "tensor") / col_norms
    return (section_out[None], grad_mag[None], grad_a[None], grad_b_acc[None], hidden_grad[None])


def solution(mesh):
    placed = (
        P("section", "tensor", None),
        P("section", None, "tensor"),
        P("section", None, None),
        P("section", None),
        P("section", None, "tensor"),
        P("section", "tensor", None),
        P("tensor", None),
        P("section", None, "tensor"),
        P("section", "tensor", None),
        P("tensor", None),
    )
    return jax.shard_map(
        local,
        mesh=mesh,
        in_specs=placed,
        out_specs=(
            P("section", "tensor", None),
            P("section", None),
            P("section", None, "tensor"),
            P("section", None, None),
            P("section", None, "tensor"),
        ),
        check_vma=False,
    )
```

profile of v0, /device:TPU:1, one launch (start us, length us, event | category | flops | bytes accessed | tf_op | source)
XLA Modules:
  0.0 220.1 jit_solution(7242099458020499546)
XLA Ops:
  7.2 0.0 reduce-scatter.5.cloned.1.call-start
  7.2 4.0 %collective-permute-start.2 = (bf16[8,896]{1,0:T(8,128)(2,1)}, bf16[8,896]{1,0:T(8,128)(2,1)S(1)}, u32[]{:S(2)}, u32[]{:S(2)}) collective-permute-start(bf16[8,896]{1,0:T(8,128)(2,1)} %bitcast.37), channel_id=1, source_target_pairs={{0,16},{16,0},{32,48},{48,32},{64,80},{80,64},{96,112},{112,96},{1... | collective-permute-start | bytes 43016 | tf_op jit(solution)/shard_map/ppermute | solution.py:10
  11.3 1.9 collective-permute-start.4
  13.2 0.7 broadcast_select_fusion.5
  14.0 3.4 %multiply_reduce_fusion = (f32[2048]{0:T(1024)S(1)}, bf16[896,2048]{1,0:T(8,128)(2,1)S(1)}) fusion(bf16[1,16,2048]{2,1,0:T(8,128)(2,1)S(1)} %copy-done, bf16[8,896]{1,0:T(8,128)(2,1)S(1)} %get-tuple-element.15, bf16[8,896]{1,0:T(8,128)(2,1)S(1)} %get-tuple-element.14, bf16[1,896,2048]{2,1,0:T(8,128)(2,1)} %param.10), kind=kOutput, calls=%fused_computation.2 | convolution fusion | flops 69785600 | bytes 7442432 | tf_op jit(solution)/shard_map/rf,rd->fd/dot_general | solution.py:74
  17.3 0.9 collective-permute-done.4
  18.3 0.8 copy-done.1
  19.1 2.6 %fusion.8 = f32[256,2048]{1,0:T(8,128)} fusion(bf16[896,2048]{1,0:T(8,128)(2,1)S(1)} %get-tuple-element.19, bf16[128,896]{1,0:T(8,128)(2,1)S(1)} %get-tuple-element.13, bf16[128,896]{1,0:T(8,128)(2,1)S(1)} %get-tuple-element.12), kind=kOutput, calls=%fused_computation.20 | convolution fusion | flops 940441600 | bytes 6225920 | tf_op jit(solution)/shard_map/dot_general | solution.py:109
  21.8 0.0 all-gather.2.cloned.1.call-start
  21.9 1.3 collective-permute-start.3
  23.2 5.1 %collective-permute-done.3 = bf16[16,2048]{1,0:T(8,128)(2,1)S(1)} collective-permute-done((bf16[16,2048]{1,0:T(8,128)(2,1)S(1)}, bf16[16,2048]{1,0:T(8,128)(2,1)S(1)}, u32[]{:S(2)}, u32[]{:S(2)}) %collective-permute-start.3) | collective-permute-done | bytes 65568 | tf_op jit(solution)/shard_map/ppermute | solution.py:16
  28.2 58.9 %reduce-scatter.5.cloned.1.call-done = f32[16,2048]{1,0:T(8,128)} async-done(((f32[256,2048]{1,0:T(8,128)}), f32[16,2048]{1,0:T(8,128)}) %reduce-scatter.5.cloned.1.call-update) | async-done | bytes 131088 | tf_op jit(solution)/shard_map/reduce_scatter | solution.py:108
  87.1 1.6 multiply_reduce_fusion.1
  88.7 0.0 reduce-scatter.3.cloned.1.call-start
  88.8 3.2 %collective-permute-start.1 = (bf16[128,896]{1,0:T(8,128)(2,1)S(1)}, bf16[128,896]{1,0:T(8,128)(2,1)S(1)}, u32[]{:S(2)}, u32[]{:S(2)}) collective-permute-start(bf16[128,896]{1,0:T(8,128)(2,1)S(1)} %bitcast.36), channel_id=1, source_target_pairs={{0,16},{16,0},{32,48},{48,32},{64,80},{80,64},{96,112},{112,96},{1... | collective-permute-start | bytes 688136 | tf_op jit(solution)/shard_map/ppermute | solution.py:10
  91.9 0.2 fusion.7
  92.2 3.3 %collective-permute-done.1 = bf16[128,896]{1,0:T(8,128)(2,1)S(1)} collective-permute-done((bf16[128,896]{1,0:T(8,128)(2,1)S(1)}, bf16[128,896]{1,0:T(8,128)(2,1)S(1)}, u32[]{:S(2)}, u32[]{:S(2)}) %collective-permute-start.1) | collective-permute-done | bytes 229408 | tf_op jit(solution)/shard_map/ppermute | solution.py:10
  95.5 0.1 broadcast_select_fusion.3
  95.6 51.3 %all-reduce = (f32[2048]{0:T(1024)S(1)}, f32[2048]{0:T(1024)S(1)}, bf16[256,16]{1,0:T(8,128)(2,1)S(1)}) all-reduce(f32[2048]{0:T(1024)S(1)} %get-tuple-element.18, f32[2048]{0:T(1024)S(1)} %get-tuple-element.8, f32[256,16]{1,0:T(8,128)S(1)} %fusion.7), channel_id=1, replica_groups=mesh['section'=32,'tensor'=16] {'tensor'}, use_global_device_ids=true, to_apply=%region_1.2 | all-reduce | flops 8192 | bytes 57344 | tf_op jit(solution)/shard_map/psum | solution.py:20
  146.9 0.6 fusion.14
  147.5 4.6 %convolution_multiply_fusion = f32[256,2048]{1,0:T(8,128)} fusion(bf16[896,2048]{1,0:T(8,128)(2,1)} %copy-done.1, f32[2048]{0:T(1024)S(1)} %get-tuple-element.17, bf16[128,896]{1,0:T(8,128)(2,1)S(1)} %get-tuple-element.11, bf16[128,896]{1,0:T(8,128)(2,1)S(1)} %get-tuple-element.10), kind=kOutput, calls=%fused_computation.3 | convolution fusion | flops 940965888 | bytes 6234112 | tf_op jit(solution)/shard_map/dot_general | solution.py:84
  152.2 3.7 %fusion.1 = f32[256,896]{1,0:T(8,128)S(1)} fusion(bf16[896,2048]{1,0:T(8,128)(2,1)} %copy-done.1, bf16[256,2048]{1,0:T(8,128)(2,1)} %all-gather.2.cloned.1.call-done, f32[2048]{0:T(1024)S(1)} %get-tuple-element.17), kind=kOutput, calls=%fused_computation.7 | convolution fusion | flops 941096960 | bytes 5644288 | tf_op jit(solution)/shard_map/td,fd->tf/dot_general | solution.py:93
  156.0 2.9 %collective-permute-start.6 = (f32[128,896]{1,0:T(8,128)S(1)}, f32[128,896]{1,0:T(8,128)S(1)}, u32[]{:S(2)}, u32[]{:S(2)}) collective-permute-start(f32[128,896]{1,0:T(8,128)S(1)} %constant_dynamic-slice_fusion), channel_id=1, source_target_pairs={{0,16},{16,0},{32,48},{48,32},{64,80},{80,64},{96,112},{112,96},{1... | collective-permute-start | bytes 1376264 | tf_op jit(solution)/shard_map/ppermute | solution.py:10
  158.9 4.1 %collective-permute-start = (bf16[16,2048]{1,0:T(8,128)(2,1)}, bf16[16,2048]{1,0:T(8,128)(2,1)S(1)}, u32[]{:S(2)}, u32[]{:S(2)}) collective-permute-start(bf16[16,2048]{1,0:T(8,128)(2,1)} %bitcast), channel_id=1, source_target_pairs={{0,32},{16,48},{32,64},{48,80},{64,96},{80,112},{96,128},{112,144}... | collective-permute-start | bytes 196616 | tf_op jit(solution)/shard_map/ppermute | solution.py:16
  163.1 0.4 fusion.2
  163.5 2.2 collective-permute-start.5
  165.7 1.0 convolution_bitcast_fusion
  166.6 1.9 collective-permute-done.5
  168.5 0.8 convolution_bitcast_fusion.1
  169.3 0.7 fusion.6
  170.0 42.0 %reduce-scatter.3.cloned.1.call-done = f32[16,2048]{1,0:T(8,128)} async-done(((f32[256,2048]{1,0:T(8,128)}), f32[16,2048]{1,0:T(8,128)}) %reduce-scatter.3.cloned.1.call-update) | async-done | bytes 131088 | tf_op jit(solution)/shard_map/reduce_scatter | solution.py:24
  212.1 1.6 fusion.9
  (24 shorter events, 0.2 us)
Async XLA Ops:
  7.2 6.8 %copy-start = (bf16[1,16,2048]{2,1,0:T(8,128)(2,1)S(1)}, bf16[1,16,2048]{2,1,0:T(8,128)(2,1)}, u32[]{:S(2)}) copy-start(bf16[1,16,2048]{2,1,0:T(8,128)(2,1)} %param.12) | copy-start | bytes 196612
  7.2 79.9 %reduce-scatter.5.cloned.1.call-start = ((), (), s32[]{:S(2)}) async-start(), calls=%async_computation.3 | async-start | bytes 2228224 | tf_op jit(solution)/shard_map/reduce_scatter | solution.py:108
  7.2 6.0 %collective-permute-start.2 = (bf16[8,896]{1,0:T(8,128)(2,1)}, bf16[8,896]{1,0:T(8,128)(2,1)S(1)}, u32[]{:S(2)}, u32[]{:S(2)}) collective-permute-start(bf16[8,896]{1,0:T(8,128)(2,1)} %bitcast.37), channel_id=1, source_target_pairs={{0,16},{16,0},{32,48},{48,32},{64,80},{80,64},{96,112},{112,96},{1... | collective-permute-start | bytes 43016 | tf_op jit(solution)/shard_map/ppermute | solution.py:10
  11.3 7.0 %collective-permute-start.4 = (bf16[128,896]{1,0:T(8,128)(2,1)}, bf16[128,896]{1,0:T(8,128)(2,1)S(1)}, u32[]{:S(2)}, u32[]{:S(2)}) collective-permute-start(bf16[128,896]{1,0:T(8,128)(2,1)} %bitcast.35), channel_id=1, source_target_pairs={{0,16},{16,0},{32,48},{48,32},{64,80},{80,64},{96,112},{112,96},{1... | collective-permute-start | bytes 688136 | tf_op jit(solution)/shard_map/ppermute | solution.py:10
  13.9 4.3 %copy-start.3 = (bf16[1,128,896]{2,1,0:T(8,128)(2,1)S(1)}, bf16[1,128,896]{2,1,0:T(8,128)(2,1)}, u32[]{:S(2)}) copy-start(bf16[1,128,896]{2,1,0:T(8,128)(2,1)} %param.17) | copy-start | bytes 688132
  17.3 1.8 copy-start.1
  19.1 2.7 %copy-start.7 = (bf16[1,16,2048]{2,1,0:T(8,128)(2,1)S(1)}, bf16[1,16,2048]{2,1,0:T(8,128)(2,1)}, u32[]{:S(2)}) copy-start(bf16[1,16,2048]{2,1,0:T(8,128)(2,1)} %param.18) | copy-start | bytes 196612
  19.1 68.0 %copy-start.5 = (bf16[16,4096]{1,0:T(8,128)(2,1)S(1)}, bf16[16,4096]{1,0:T(8,128)(2,1)}, u32[]{:S(2)}) copy-start(bf16[16,4096]{1,0:T(8,128)(2,1)} %param.19) | copy-start | bytes 393220
  19.1 69.6 %copy-start.4 = (bf16[1,128,896]{2,1,0:T(8,128)(2,1)S(1)}, bf16[1,128,896]{2,1,0:T(8,128)(2,1)}, u32[]{:S(2)}) copy-start(bf16[1,128,896]{2,1,0:T(8,128)(2,1)} %param.14) | copy-start | bytes 688132
  21.8 125.1 %copy-start.6 = (f32[1,2048]{1,0:T(1,128)S(1)}, f32[1,2048]{1,0:T(1,128)}, u32[]{:S(2)}) copy-start(f32[1,2048]{1,0:T(1,128)} %param.13) | copy-start | bytes 24580
  21.8 130.4 %all-gather.2.cloned.1.call-start = ((), (), s32[]{:S(2)}) async-start(), calls=%async_computation.4 | async-start | bytes 1114112 | tf_op jit(solution)/shard_map/all_gather | solution.py:91
  21.9 6.4 %collective-permute-start.3 = (bf16[16,2048]{1,0:T(8,128)(2,1)S(1)}, bf16[16,2048]{1,0:T(8,128)(2,1)S(1)}, u32[]{:S(2)}, u32[]{:S(2)}) collective-permute-start(bf16[16,2048]{1,0:T(8,128)(2,1)S(1)} %bitcast.40), channel_id=1, source_target_pairs={{32,0},{48,16},{64,32},{80,48},{96,64},{112,80},{128,96},{144,112}... | collective-permute-start | bytes 196616 | tf_op jit(solution)/shard_map/ppermute | solution.py:16
  88.7 123.3 %reduce-scatter.3.cloned.1.call-start = ((), (), s32[]{:S(2)}) async-start(), calls=%async_computation.2 | async-start | bytes 2228224 | tf_op jit(solution)/shard_map/reduce_scatter | solution.py:24
  88.8 6.8 %collective-permute-start.1 = (bf16[128,896]{1,0:T(8,128)(2,1)S(1)}, bf16[128,896]{1,0:T(8,128)(2,1)S(1)}, u32[]{:S(2)}, u32[]{:S(2)}) collective-permute-start(bf16[128,896]{1,0:T(8,128)(2,1)S(1)} %bitcast.36), channel_id=1, source_target_pairs={{0,16},{16,0},{32,48},{48,32},{64,80},{80,64},{96,112},{112,96},{1... | collective-permute-start | bytes 688136 | tf_op jit(solution)/shard_map/ppermute | solution.py:10
  152.2 10.9 %copy-start.2 = (bf16[256,2048]{1,0:T(8,128)(2,1)S(1)}, bf16[256,2048]{1,0:T(8,128)(2,1)}, u32[]{:S(2)}) copy-start(bf16[256,2048]{1,0:T(8,128)(2,1)} %all-gather.2.cloned.1.call-done) | copy-start | bytes 3145732
  156.0 13.3 %collective-permute-start.6 = (f32[128,896]{1,0:T(8,128)S(1)}, f32[128,896]{1,0:T(8,128)S(1)}, u32[]{:S(2)}, u32[]{:S(2)}) collective-permute-start(f32[128,896]{1,0:T(8,128)S(1)} %constant_dynamic-slice_fusion), channel_id=1, source_target_pairs={{0,16},{16,0},{32,48},{48,32},{64,80},{80,64},{96,112},{112,96},{1... | collective-permute-start | bytes 1376264 | tf_op jit(solution)/shard_map/ppermute | solution.py:10
  158.9 11.1 %collective-permute-start = (bf16[16,2048]{1,0:T(8,128)(2,1)}, bf16[16,2048]{1,0:T(8,128)(2,1)S(1)}, u32[]{:S(2)}, u32[]{:S(2)}) collective-permute-start(bf16[16,2048]{1,0:T(8,128)(2,1)} %bitcast), channel_id=1, source_target_pairs={{0,32},{16,48},{32,64},{48,80},{64,96},{80,112},{96,128},{112,144}... | collective-permute-start | bytes 196616 | tf_op jit(solution)/shard_map/ppermute | solution.py:16
  163.5 5.0 %collective-permute-start.5 = (f32[256,16]{0,1:T(8,128)S(1)}, f32[256,16]{0,1:T(8,128)S(1)}, u32[]{:S(2)}, u32[]{:S(2)}) collective-permute-start(f32[256,16]{0,1:T(8,128)S(1)} %fusion.2), channel_id=1, source_target_pairs={{0,16},{16,0},{32,48},{48,32},{64,80},{80,64},{96,112},{112,96},{1... | collective-permute-start | bytes 49160 | tf_op jit(solution)/shard_map/ppermute | solution.py:10
Sparse Core Ops, SparseCore 0:
  21.9 65.1 reduce-scatter.4
  89.8 43.1 all-gather.1
  152.3 59.7 reduce-scatter.2
where the time goes:
time: 223 us; the launch traced here: 220 us
  waiting for transfers between devices  112 us (50%)
  blocking collectives  51.3 us (23%)
  starting transfers between devices  19.8 us (9%)
  matrix products  16.7 us (7%)
  between operations  14 us (6%)
  other arithmetic  5.3 us (2%)
    reduce_scatter x1, waiting for transfers between devices, local(): lax.psum_scatter(jnp.dot(hid_bwd, merged, preferred_element_type=jnp.floa...  58.9 us
    psum x1, blocking collectives, column_norms(): return jnp.sqrt(lax.psum(squares, 'tensor') + epsilon)  51.3 us
    reduce_scatter x1, waiting for transfers between devices, forward_rows(): lax.psum_scatter(term_fn(jnp.int32(0), own_rows * lax.axis_size('tensor')...  42 us
    ppermute x5, starting transfers between devices, swapped(): lax.ppermute(array, axis, [(i, i ^ 1 << apart) for i in range(lax.axis_si...  14.2 us
    ppermute x5, waiting for transfers between devices, swapped(): lax.ppermute(array, axis, [(i, i ^ 1 << apart) for i in range(lax.axis_si...  6.13 us
    ppermute x2, starting transfers between devices, from_behind(): return lax.ppermute(array, axis, pairs)  5.41 us
    ppermute x2, waiting for transfers between devices, from_behind(): return lax.ppermute(array, axis, pairs)  5.06 us
    dot_general x1, matrix products, scaled_term(): jnp.dot(hid_fwd, merged, preferred_element_type=jnp.float32) * col_scale  4.63 us
  transfers between devices with their start and end apart: 10, of which 6 were waited for; matrix products, arithmetic and copies ran while one was open for 7% of the time, Pallas kernels for 0%

commit v1 on v0

v1 whole, which is shorter than its diff:
```python
import jax
import jax.numpy as jnp
from jax import lax
from jax.experimental import pallas as pl
from jax.experimental.pallas import tpu as pltpu
from jax.sharding import PartitionSpec as P

epsilon = 1e-06
bf16 = jnp.bfloat16
f32 = jnp.float32


def dot(left, right, left_dim, right_dim):
    return lax.dot_general(
        left, right, (((left_dim,), (right_dim,)), ((), ())), preferred_element_type=f32
    )


def make_kernel(secs, tens, names, n_sems):
    rings = tens // 2
    far = rings // 2

    def kernel(*refs):
        (w_in, a_in, b_in, mag_in, hf_in, car_in, emb_in, hb_in, ret_in, head_in) = refs[:10]
        (so_out, gm_out, ga_out, gb_out, hg_out) = refs[10:15]
        s = dict(zip(names, refs[15:]))
        w, a_own, a_oth, b, mag = s["w"], s["a_own"], s["a_oth"], s["b"], s["mag"]
        xf, xb, infl, cot, scot = s["xf"], s["xb"], s["infl"], s["cot"], s["scot"]
        sems = s["sems"]
        used = [0]

        def sem():
            used[0] += 1
            assert used[0] <= n_sems
            return sems.at[used[0] - 1]

        depth, width = w.shape
        wide = width // 2
        half_rows = xb.shape[1]
        blocks = half_rows // 16

        sec = lax.axis_index("section")
        ten = lax.axis_index("tensor")
        half = lax.rem(sec, 2)
        core = lax.rem(ten, 2)
        z = ten // 2
        partner = {"section": sec + 1 - 2 * half}
        sibling = {"tensor": ten + 1 - 2 * core}
        next_sec = {"section": lax.rem(sec + 2, secs)}
        prev_sec = {"section": lax.rem(sec + secs - 2, secs)}
        up = {"tensor": lax.rem(ten + 2, tens)}
        down = {"tensor": lax.rem(ten + tens - 2, tens)}

        def remote(src, dst, where):
            return pltpu.make_async_remote_copy(
                src_ref=src,
                dst_ref=dst,
                send_sem=sem(),
                recv_sem=sem(),
                device_id=where,
                device_id_type=pl.DeviceIdType.MESH,
            )

        def local(src, dst):
            return pltpu.make_async_copy(src, dst, sem())

        def cols(q):
            return pl.ds(q * wide, wide)

        sent = []

        def start(*copies):
            for copy in copies:
                copy.start()
                sent.append(copy)

        ld_a = local(a_in.at[0], a_own)
        ld_b = local(b_in.at[0], b)
        ld_w = local(w_in.at[0], w)
        ld_mag = local(mag_in, mag)
        ld_hb = local(hb_in.at[0], xb.at[half])
        ld_hf = [local(hf_in.at[:, p], xf.at[p, pl.ds(half * (blocks // 2), blocks // 2)]) for p in (0, 1)]
        own_cols = pl.ds(pl.multiple_of(half * width, 128), width)
        ld_infl = local(emb_in.at[:, own_cols], infl)
        ld_cot = local(head_in.at[:, own_cols], cot.at[ten])
        for copy in (ld_a, ld_b, ld_w, ld_hb, ld_mag, *ld_hf):
            copy.start()

        @pl.when(sec < 2)
        def _():
            ld_infl.start()

        @pl.when(sec >= secs - 2)
        def _():
            ld_cot.start()

        barrier = pltpu.get_barrier_semaphore()
        peers = [{"tensor": lax.rem(ten + k, tens)} for k in range(1, tens)]
        everyone = [partner, next_sec, prev_sec] + peers
        for where in everyone:
            pl.semaphore_signal(barrier, inc=1, device_id=where, device_id_type=pl.DeviceIdType.MESH)
        pl.semaphore_wait(barrier, len(everyone))

        sw_a = remote(a_in.at[0], a_oth, partner)
        sw_ret = remote(ret_in.at[0], cot.at[ten], prev_sec)
        sw_hf = [
            remote(hf_in.at[:, p], xf.at[p, pl.ds(half * (blocks // 2), blocks // 2)], partner)
            for p in (0, 1)
        ]
        sw_hb = remote(hb_in.at[0], xb.at[half], partner)
        sw_car = remote(car_in.at[0], infl, next_sec)
        start(sw_a)

        @pl.when(sec >= 2)
        def _():
            sw_ret.start()

        start(*sw_hf, sw_hb)

        @pl.when(sec < secs - 2)
        def _():
            sw_car.start()

        def block(zz):
            return lax.rem(zz + rings, rings) * 2 + core

        def gather_copy(k, q, sign, where):
            ref = cot.at[block(z - sign * (k - 1)), :, cols(q)]
            return remote(ref, ref, where)

        ag_up = {(k, q): gather_copy(k, q, 1, up) for k in range(1, far + 1) for q in (0, 1) if k < far or q == 0}
        ag_dn = {(k, q): gather_copy(k, q, -1, down) for k in range(1, far + 1) for q in (0, 1) if k < far or q == 1}

        def cross(zz, q=None):
            ref = cot.at[block(zz)] if q is None else cot.at[block(zz), :, cols(q)]
            return remote(ref, ref, sibling)

        ag_x = [cross(z)]

        def gather_first():
            @pl.when(sec < secs - 2)
            def _():
                sw_ret.wait_recv()

            @pl.when(sec >= secs - 2)
            def _():
                ld_cot.wait()

            for q in (0, 1):
                for ag in (ag_up, ag_dn):
                    if (1, q) in ag:
                        start(ag[1, q])
            start(ag_x[0])

        def gather_step(k):
            for q in (0, 1):
                for ag in (ag_up, ag_dn):
                    if (k, q) in ag:
                        ag[k, q].wait_recv()
                        if (k + 1, q) in ag:
                            start(ag[k + 1, q])
            if k < far:
                more = [cross(z - k), cross(z + k)]
            else:
                more = [cross(z - k, 0), cross(z + k, 1)]
            start(*more)
            ag_x.extend(more)

        def total_of(part, sib, slots, own_half):
            first = remote(part, sib, sibling)

            def stage1():
                start(first)

            copies = []

            def stage2():
                first.wait_recv()
                slots[z] = part[...] + sib[...]
                ref = slots.at[(z, *own_half)]
                for k in range(1, rings):
                    for other in (0, 1):
                        there = lax.rem(z + k, rings) * 2 + (core if other == 0 else 1 - core)
                        copies.append(remote(ref, ref, {"tensor": there}))
                start(*copies)

            def stage3():
                for copy in copies:
                    copy.wait_recv()
                total = slots[0]
                for k in range(1, rings):
                    total = total + slots[k]
                return total

            return stage1, stage2, stage3

        lane_half = (slice(None), pl.ds(pl.multiple_of(core * wide, 128), wide))
        row_half = (pl.ds(pl.multiple_of(core * 8, 8), 8), slice(None))
        sq1, sq2, sq3 = total_of(s["sq"], s["sq_sib"], s["sq_slots"], lane_half)
        gm1, gm2, gm3 = total_of(s["gmp"], s["gm_sib"], s["gm_slots"], lane_half)
        lo1, lo2, lo3 = total_of(s["lo"], s["lo_sib"], s["lo_slots"], row_half)

        ld_a.wait()
        ld_b.wait()
        ld_hb.wait()
        sw_a.wait_recv()
        mine, theirs = a_own[...].astype(f32), a_oth[...].astype(f32)
        first = half == 0
        a_all = jnp.concatenate(
            [jnp.where(first, mine, theirs), jnp.where(first, theirs, mine)], axis=0
        )
        s["at"][...] = a_all.T.astype(bf16)
        s["lo"][...] = dot(a_all.astype(bf16), xb[half], 1, 1)
        lo1()

        step_cols = min(256, width)
        step_rows = min(128, depth)

        def merge(i, carry):
            cc = pl.ds(pl.multiple_of(i * step_cols, step_cols), step_cols)
            b_c = b[:, cc]
            total = jnp.zeros((8, step_cols), f32)
            for r in range(0, depth, step_rows):
                rr = pl.ds(r, step_rows)
                m = (w[rr, cc].astype(f32) + dot(s["at"][rr, :], b_c, 1, 0)).astype(bf16)
                w[rr, cc] = m
                m = m.astype(f32)
                total = total + jnp.sum((m * m).reshape(step_rows // 8, 8, step_cols), axis=0)
            s["sq"][:, cc] = jnp.sum(total, axis=0, keepdims=True)
            return carry

        ld_w.wait()
        n_merge = width // step_cols
        lax.fori_loop(0, n_merge // 2, merge, 0)
        gather_first()
        lo2()
        lax.fori_loop(n_merge // 2, n_merge, merge, 0)
        sq1()
        gather_step(1)
        sq2()
        low_own = lo3().astype(bf16)
        s["low_own"][...] = low_own
        sw_low = remote(s["low_own"], s["low_oth"], partner)
        start(sw_low)
        if far > 2:
            gather_step(2)

        for copy in ld_hf:
            copy.wait()
        for copy in sw_hf:
            copy.wait_recv()
        pcols = min(512, width)

        def project(parity, keep):
            def body(i, carry):
                cc = pl.ds(pl.multiple_of(i * pcols, pcols), pcols)
                x = xf[parity].reshape(half_rows, depth)
                res = dot(x, w[:, cc], 1, 0)
                keep[:, :, cc] = res.reshape(rings, 16, pcols).astype(keep.dtype)
                return carry

            lax.fori_loop(0, width // pcols, body, 0)

        project(1 - core, s["p_send"])
        sw_p = remote(s["p_send"], s["p_recv"], sibling)
        start(sw_p)
        for k in range(3 if far > 2 else 2, far):
            gather_step(k)
        project(core, s["pm"])
        gather_step(far)

        ld_mag.wait()
        norms = jnp.sqrt(sq3() + epsilon)
        s["norms"][...] = norms
        s["scale"][...] = mag[...] / norms
        for copy in ag_x:
            copy.wait_recv()

        def rescale(i, carry):
            scot[i] = (cot[i].astype(f32) * s["scale"][...]).astype(bf16)
            return carry

        lax.fori_loop(0, tens, rescale, 0)

        hsplit = [(0, depth)] if depth < 896 else [(0, 512), (512, depth - 512)]

        def hidden(which, lo, size):
            rows = scot[pl.ds(which * blocks, blocks)].reshape(half_rows, width)
            return dot(rows, w[pl.ds(lo, size), :], 1, 1)

        sw_hg = []
        for lo, size in hsplit:
            s["hg_send"][:, pl.ds(lo, size)] = hidden(1 - half, lo, size).astype(bf16)
            copy = remote(s["hg_send"].at[:, pl.ds(lo, size)], s["hg_recv"].at[:, pl.ds(lo, size)], partner)
            start(copy)
            sw_hg.append(copy)

        adapt = dot(b[...], scot[...].reshape(2 * half_rows, width), 1, 1)
        s["ad"][...] = adapt.reshape(2, 8, 2 * half_rows)
        sw_ad = remote(s["ad"].at[1 - half], s["ad_recv"], partner)
        start(sw_ad)

        pm = s["pm"]
        sw_p.wait_recv()

        def merge_cores(i, carry):
            pm[i] = pm[i] + s["p_recv"][i].astype(f32)
            return carry

        lax.fori_loop(0, rings, merge_cores, 0)
        rs = {}

        def scatter_step(k):
            for q in (0, 1):
                for name, sign, first_q, where in (("u", 1, 0, up), ("d", -1, 1, down)):
                    if k == 1 and q != first_q:
                        continue
                    dest = lax.rem(z + sign * (far + 1 - k) + rings, rings)
                    val = pm[dest, :, cols(q)]
                    if (name, k - 1, q) in rs:
                        rs[name, k - 1, q].wait_recv()
                        val = val + s["rs_recv_" + name][k - 2, :, cols(q)].astype(f32)
                    s["rs_send_" + name][k - 1, :, cols(q)] = val.astype(bf16)
                    copy = remote(
                        s["rs_send_" + name].at[k - 1, :, cols(q)],
                        s["rs_recv_" + name].at[k - 1, :, cols(q)],
                        where,
                    )
                    start(copy)
                    rs[name, k, q] = copy

        scatter_step(1)

        for i, (lo, size) in enumerate(hsplit):
            s["hg_own"][:, pl.ds(lo, size)] = hidden(half, lo, size)
        scatter_step(2)

        sw_hb.wait_recv()

        def recompute(i, carry):
            cc = pl.ds(pl.multiple_of(i * step_cols, step_cols), step_cols)
            res = dot(xb[...].reshape(2 * half_rows, depth), w[:, cc], 1, 0)
            got = cot[:, :, cc].reshape(2 * half_rows, step_cols).astype(f32)
            part = jnp.sum((res * got).reshape(half_rows // 4, 8, step_cols), axis=0)
            s["gmp"][:, cc] = jnp.sum(part, axis=0, keepdims=True)
            return carry

        n_rec = width // step_cols
        lax.fori_loop(0, n_rec // 2, recompute, 0)
        if far > 2:
            scatter_step(3)
        lax.fori_loop(n_rec // 2, n_rec, recompute, 0)
        gm1()
        for k in range(4 if far > 2 else 3, far + 1):
            scatter_step(k)
        gm2()

        sw_ad.wait_recv()
        own_ad = (s["ad"][half] + s["ad_recv"][...]).astype(bf16)
        s["ga"][...] = dot(own_ad, xb[...].reshape(2 * half_rows, depth), 1, 0)
        out_ga = local(s["ga"], ga_out.at[0])
        out_ga.start()
        sw_low.wait_recv()
        s["gb"][...] = dot(
            s["low_own"][...], scot[pl.ds(half * blocks, blocks)].reshape(half_rows, width), 1, 0
        ) + dot(
            s["low_oth"][...], scot[pl.ds((1 - half) * blocks, blocks)].reshape(half_rows, width), 1, 0
        )
        out_gb = local(s["gb"], gb_out.at[0])
        out_gb.start()

        @pl.when(sec < 2)
        def _():
            ld_infl.wait()

        @pl.when(sec >= 2)
        def _():
            sw_car.wait_recv()

        for q in (0, 1):
            val = pm[z, :, cols(q)]
            for name in "ud":
                if (name, far, q) in rs:
                    rs[name, far, q].wait_recv()
                    val = val + s["rs_recv_" + name][far - 1, :, cols(q)].astype(f32)
            val = infl[:, cols(q)].astype(f32) + val * s["scale"][:, cols(q)]
            s["so"][:, cols(q)] = val.astype(bf16)
        out_so = local(s["so"], so_out.at[0])
        out_so.start()

        s["gm"][...] = gm3() / s["norms"][...]
        out_gm = local(s["gm"], gm_out)
        out_gm.start()

        for copy in sw_hg:
            copy.wait_recv()
        s["hg"][...] = (s["hg_own"][...] + s["hg_recv"][...].astype(f32)).astype(bf16)
        out_hg = local(s["hg"], hg_out.at[0])
        out_hg.start()

        for copy in sent:
            copy.wait_send()

        @pl.when(sec >= 2)
        def _():
            sw_ret.wait_send()

        @pl.when(sec < secs - 2)
        def _():
            sw_car.wait_send()

        for copy in (out_ga, out_gb, out_so, out_gm, out_hg):
            copy.wait()

    return kernel


def local(secs, tens, *args):
    (frozen, adapter_a, adapter_b, magnitude, hidden_fwd, carried, embedded, hidden_bwd, returned, head) = args
    depth, width = frozen.shape[1:]
    half_rows = hidden_fwd.shape[1]
    rings = tens // 2
    far = rings // 2
    n_sems = 320
    shapes = {
        "w": pltpu.VMEM((depth, width), bf16),
        "a_own": pltpu.VMEM((8, depth), bf16),
        "a_oth": pltpu.VMEM((8, depth), bf16),
        "at": pltpu.VMEM((depth, 16), bf16),
        "b": pltpu.VMEM((16, width), bf16),
        "mag": pltpu.VMEM((1, width), f32),
        "norms": pltpu.VMEM((1, width), f32),
        "scale": pltpu.VMEM((1, width), f32),
        "xf": pltpu.VMEM((2, rings, 16, depth), bf16),
        "xb": pltpu.VMEM((2, half_rows, depth), bf16),
        "infl": pltpu.VMEM((16, width), bf16),
        "cot": pltpu.VMEM((tens, 16, width), bf16),
        "scot": pltpu.VMEM((tens, 16, width), bf16),
        "sq": pltpu.VMEM((1, width), f32),
        "sq_sib": pltpu.VMEM((1, width), f32),
        "sq_slots": pltpu.VMEM((rings, 1, width), f32),
        "gmp": pltpu.VMEM((1, width), f32),
        "gm_sib": pltpu.VMEM((1, width), f32),
        "gm_slots": pltpu.VMEM((rings, 1, width), f32),
        "lo": pltpu.VMEM((16, half_rows), f32),
        "lo_sib": pltpu.VMEM((16, half_rows), f32),
        "lo_slots": pltpu.VMEM((rings, 16, half_rows), f32),
        "low_own": pltpu.VMEM((16, half_rows), bf16),
        "low_oth": pltpu.VMEM((16, half_rows), bf16),
        "p_send": pltpu.VMEM((rings, 16, width), bf16),
        "p_recv": pltpu.VMEM((rings, 16, width), bf16),
        "pm": pltpu.VMEM((rings, 16, width), f32),
        "rs_send_u": pltpu.VMEM((far, 16, width), bf16),
        "rs_recv_u": pltpu.VMEM((far, 16, width), bf16),
        "rs_send_d": pltpu.VMEM((far, 16, width), bf16),
        "rs_recv_d": pltpu.VMEM((far, 16, width), bf16),
        "hg_send": pltpu.VMEM((half_rows, depth), bf16),
        "hg_recv": pltpu.VMEM((half_rows, depth), bf16),
        "hg_own": pltpu.VMEM((half_rows, depth), f32),
        "ad": pltpu.VMEM((2, 8, 2 * half_rows), f32),
        "ad_recv": pltpu.VMEM((8, 2 * half_rows), f32),
        "so": pltpu.VMEM((16, width), bf16),
        "gm": pltpu.VMEM((1, width), f32),
        "ga": pltpu.VMEM((8, depth), f32),
        "gb": pltpu.VMEM((16, width), f32),
        "hg": pltpu.VMEM((half_rows, depth), bf16),
        "sems": pltpu.SemaphoreType.DMA((n_sems,)),
    }
    anywhere = pl.BlockSpec(memory_space=pl.ANY)
    return pl.pallas_call(
        make_kernel(secs, tens, list(shapes), n_sems),
        out_shape=(
            jax.ShapeDtypeStruct((1, 16, width), bf16),
            jax.ShapeDtypeStruct((1, width), f32),
            jax.ShapeDtypeStruct((1, 8, depth), f32),
            jax.ShapeDtypeStruct((1, 16, width), f32),
            jax.ShapeDtypeStruct((1, half_rows, depth), bf16),
        ),
        in_specs=[anywhere] * 10,
        out_specs=(anywhere,) * 5,
        scratch_shapes=list(shapes.values()),
        compiler_params=pltpu.CompilerParams(
            collective_id=0, has_side_effects=True, vmem_limit_bytes=48 * 1024 * 1024
        ),
    )(
        frozen,
        adapter_a,
        adapter_b,
        magnitude,
        hidden_fwd.reshape(half_rows // 32, 2, 16, depth),
        carried,
        embedded,
        hidden_bwd,
        returned,
        head,
    )


def solution(mesh):
    secs, tens = mesh.shape["section"], mesh.shape["tensor"]
    placed = (
        P("section", "tensor", None),
        P("section", None, "tensor"),
        P("section", None, None),
        P("section", None),
        P("section", None, "tensor"),
        P("section", "tensor", None),
        P("tensor", None),
        P("section", None, "tensor"),
        P("section", "tensor", None),
        P("tensor", None),
    )

    def run(*args):
        return local(secs, tens, *args)

    return jax.shard_map(
        run,
        mesh=mesh,
        in_specs=placed,
        out_specs=(
            P("section", "tensor", None),
            P("section", None),
            P("section", None, "tensor"),
            P("section", None, None),
            P("section", None, "tensor"),
        ),
        check_vma=False,
    )
```

time: 223 us -> 71.1 us (0.32); the launches traced: 220 us -> 70.6 us
  waiting for transfers between devices: 112 us -> 0 us
  Pallas kernels: 0 us -> 57.1 us
  blocking collectives: 51.3 us -> 0 us
  starting transfers between devices: 19.8 us -> 0 us
  matrix products: 16.7 us -> 0 us
  between operations: 14 us -> 0.66 us
  local copies, waits for them, and re-layouts: 0.89 us -> 12.8 us
  other arithmetic: 5.3 us -> 0 us
    reduce_scatter x2 -> x0, waiting for transfers between devices: 101 us -> none  [the longest x1 58.9 us: local(): lax.psum_scatter(jnp.dot(hid_bwd, merged, preferred_element_type=jnp.floa...]
    pallas_call x0 -> x1, Pallas kernels: none -> 57.1 us  [local(): pl.pallas_call(make_kernel(secs, tens, list(shapes), n_sems), out_shape=(...]
    psum x1 -> x0, blocking collectives: 51.3 us -> none  [column_norms(): return jnp.sqrt(lax.psum(squares, 'tensor') + epsilon)]
    ppermute x7 -> x0, starting transfers between devices: 19.6 us -> none  [the longest x5 14.2 us: swapped(): lax.ppermute(array, axis, [(i, i ^ 1 << apart) for i in range(lax.axis_si...]
    dot_general x8 -> x0, matrix products: 16.7 us -> none  [the longest x1 4.63 us: scaled_term(): jnp.dot(hid_fwd, merged, preferred_element_type=jnp.float32) * col_scale]
    unnamed x16 -> x25, local copies, waits for them, and re-layouts: 0.85 us -> 12.8 us
    ppermute x7 -> x0, waiting for transfers between devices: 11.2 us -> none  [the longest x5 6.13 us: swapped(): lax.ppermute(array, axis, [(i, i ^ 1 << apart) for i in range(lax.axis_si...]
    broadcast_in_dim x2 -> x0, other arithmetic: 2.3 us -> none  [the longest x1 1.56 us: local(): section_out[None]]
  transfers between devices with their start and end apart: 10 -> 0, of which waited for: 6 -> 0; matrix products, arithmetic and copies ran while one was open for 7% -> 0% of each run, Pallas kernels for 0% -> 0%
where the time goes in v1:
time: 71.1 us; the launch traced here: 70.6 us
  Pallas kernels  57.1 us (80%)
  local copies, waits for them, and re-layouts  12.8 us (18%)
    pallas_call x1, Pallas kernels, local(): pl.pallas_call(make_kernel(secs, tens, list(shapes), n_sems), out_shape=(...  57.1 us
    unnamed x25, local copies, waits for them, and re-layouts  12.8 us

profile of v1, /device:TPU:1, one launch (start us, length us, event | category | flops | bytes accessed | tf_op | source)
XLA Modules:
  0.0 70.6 jit_solution(15469044860996372649)
XLA Ops:
  0.6 0.0 copy-start
  0.6 2.0 %copy-done = bf16[1,896,2048]{2,1,0:T(8,128)(2,1)S(1)} copy-done((bf16[1,896,2048]{2,1,0:T(8,128)(2,1)S(1)}, bf16[1,896,2048]{2,1,0:T(8,128)(2,1)}, u32[]{:S(2)}) %copy-start) | copy-done | bytes 3670040
  2.7 0.0 copy-start.1
  2.7 0.9 %copy-done.1 = bf16[1,128,896]{2,1,0:T(8,128)(2,1)S(1)} copy-done((bf16[1,128,896]{2,1,0:T(8,128)(2,1)S(1)}, bf16[1,128,896]{2,1,0:T(8,128)(2,1)}, u32[]{:S(2)}) %copy-start.1) | copy-done | bytes 229400
  3.6 0.0 copy-start.2
  3.6 0.9 %copy-done.2 = bf16[1,128,896]{2,1,0:T(8,128)(2,1)S(1)} copy-done((bf16[1,128,896]{2,1,0:T(8,128)(2,1)S(1)}, bf16[1,128,896]{2,1,0:T(8,128)(2,1)}, u32[]{:S(2)}) %copy-start.2) | copy-done | bytes 229400
  4.6 0.0 copy-start.3
  4.6 0.9 %copy-done.3 = bf16[16,4096]{1,0:T(8,128)(2,1)S(1)} copy-done((bf16[16,4096]{1,0:T(8,128)(2,1)S(1)}, bf16[16,4096]{1,0:T(8,128)(2,1)}, u32[]{:S(2)}) %copy-start.3) | copy-done | bytes 131096
  5.5 0.0 copy-start.4
  5.5 0.9 %copy-done.4 = bf16[16,4096]{1,0:T(8,128)(2,1)S(1)} copy-done((bf16[16,4096]{1,0:T(8,128)(2,1)S(1)}, bf16[16,4096]{1,0:T(8,128)(2,1)}, u32[]{:S(2)}) %copy-start.4) | copy-done | bytes 131096
  6.4 0.0 copy-start.5
  6.4 0.8 %copy-done.5 = bf16[1,16,2048]{2,1,0:T(8,128)(2,1)S(1)} copy-done((bf16[1,16,2048]{2,1,0:T(8,128)(2,1)S(1)}, bf16[1,16,2048]{2,1,0:T(8,128)(2,1)}, u32[]{:S(2)}) %copy-start.5) | copy-done | bytes 65560
  7.2 0.0 copy-start.6
  7.2 0.8 %copy-done.6 = bf16[1,16,2048]{2,1,0:T(8,128)(2,1)S(1)} copy-done((bf16[1,16,2048]{2,1,0:T(8,128)(2,1)S(1)}, bf16[1,16,2048]{2,1,0:T(8,128)(2,1)}, u32[]{:S(2)}) %copy-start.6) | copy-done | bytes 65560
  8.0 0.0 copy-start.7
  8.0 0.8 %copy-done.7 = bf16[1,16,2048]{2,1,0:T(8,128)(2,1)S(1)} copy-done((bf16[1,16,2048]{2,1,0:T(8,128)(2,1)S(1)}, bf16[1,16,2048]{2,1,0:T(8,128)(2,1)}, u32[]{:S(2)}) %copy-start.7) | copy-done | bytes 65560
  8.9 0.0 copy-start.8
  8.9 0.7 %copy-done.8 = bf16[1,8,896]{2,1,0:T(8,128)(2,1)S(1)} copy-done((bf16[1,8,896]{2,1,0:T(8,128)(2,1)S(1)}, bf16[1,8,896]{2,1,0:T(8,128)(2,1)}, u32[]{:S(2)}) %copy-start.8) | copy-done | bytes 14360
  9.6 0.0 copy-start.9
  9.6 0.7 copy-done.9
  10.3 57.1 %shard_map.137 = (bf16[1,16,2048]{2,1,0:T(8,128)(2,1)S(1)}, f32[1,2048]{1,0:T(1,128)S(1)}, f32[1,8,896]{2,1,0:T(8,128)S(1)}, f32[1,16,2048]{2,1,0:T(8,128)S(1)}, bf16[1,128,896]{2,1,0:T(8,128)(2,1)S(1)}) custom-call(bf16[1,896,2048]{2,1,0:T(8,128)(2,1)S(1)} %copy-done, bf16[1,8,896]{2,1,0:T(8,128)(2,1)S(1)} %copy-done.8, bf16[1,16,2048]{2,1,0:T(8,128)(2,1)S(1)} %copy-done.5, ...), custom_call_target="tpu_custom_call" | custom-call | tf_op jit(solution)/shard_map/pallas_call | solution.py:470
  67.4 0.6 copy.20
  68.1 0.6 copy.21
  68.7 0.6 copy.22
  69.3 0.7 copy.23
  69.9 0.7 copy.24
Async XLA Ops:
  0.6 2.0 %copy-start = (bf16[1,896,2048]{2,1,0:T(8,128)(2,1)S(1)}, bf16[1,896,2048]{2,1,0:T(8,128)(2,1)}, u32[]{:S(2)}) copy-start(bf16[1,896,2048]{2,1,0:T(8,128)(2,1)} %refs_0_.1) | copy-start | bytes 11010052
  2.7 0.9 %copy-start.1 = (bf16[1,128,896]{2,1,0:T(8,128)(2,1)S(1)}, bf16[1,128,896]{2,1,0:T(8,128)(2,1)}, u32[]{:S(2)}) copy-start(bf16[1,128,896]{2,1,0:T(8,128)(2,1)} %param.14) | copy-start | bytes 688132
  3.6 0.9 %copy-start.2 = (bf16[1,128,896]{2,1,0:T(8,128)(2,1)S(1)}, bf16[1,128,896]{2,1,0:T(8,128)(2,1)}, u32[]{:S(2)}) copy-start(bf16[1,128,896]{2,1,0:T(8,128)(2,1)} %refs_7_.1) | copy-start | bytes 688132
  4.6 0.9 %copy-start.3 = (bf16[16,4096]{1,0:T(8,128)(2,1)S(1)}, bf16[16,4096]{1,0:T(8,128)(2,1)}, u32[]{:S(2)}) copy-start(bf16[16,4096]{1,0:T(8,128)(2,1)} %refs_6_.1) | copy-start | bytes 393220
  5.5 0.9 %copy-start.4 = (bf16[16,4096]{1,0:T(8,128)(2,1)S(1)}, bf16[16,4096]{1,0:T(8,128)(2,1)}, u32[]{:S(2)}) copy-start(bf16[16,4096]{1,0:T(8,128)(2,1)} %refs_9_.1) | copy-start | bytes 393220
  6.4 0.8 %copy-start.5 = (bf16[1,16,2048]{2,1,0:T(8,128)(2,1)S(1)}, bf16[1,16,2048]{2,1,0:T(8,128)(2,1)}, u32[]{:S(2)}) copy-start(bf16[1,16,2048]{2,1,0:T(8,128)(2,1)} %refs_2_.1) | copy-start | bytes 196612
  7.2 0.8 %copy-start.6 = (bf16[1,16,2048]{2,1,0:T(8,128)(2,1)S(1)}, bf16[1,16,2048]{2,1,0:T(8,128)(2,1)}, u32[]{:S(2)}) copy-start(bf16[1,16,2048]{2,1,0:T(8,128)(2,1)} %refs_5_.1) | copy-start | bytes 196612
  8.0 0.8 %copy-start.7 = (bf16[1,16,2048]{2,1,0:T(8,128)(2,1)S(1)}, bf16[1,16,2048]{2,1,0:T(8,128)(2,1)}, u32[]{:S(2)}) copy-start(bf16[1,16,2048]{2,1,0:T(8,128)(2,1)} %refs_8_.1) | copy-start | bytes 196612
  8.9 0.7 %copy-start.8 = (bf16[1,8,896]{2,1,0:T(8,128)(2,1)S(1)}, bf16[1,8,896]{2,1,0:T(8,128)(2,1)}, u32[]{:S(2)}) copy-start(bf16[1,8,896]{2,1,0:T(8,128)(2,1)} %refs_1_.1) | copy-start | bytes 43012
  9.6 0.7 copy-start.9

commit v2 on v1

--- a/solution.py
+++ b/solution.py
@@ -18,7 +18,7 @@
 
 def make_kernel(secs, tens, names, n_sems):
     rings = tens // 2
-    far = rings // 2
+    assert rings == 8
 
     def kernel(*refs):
         (w_in, a_in, b_in, mag_in, hf_in, car_in, emb_in, hb_in, ret_in, head_in) = refs[:10]
@@ -48,8 +48,6 @@
         sibling = {"tensor": ten + 1 - 2 * core}
         next_sec = {"section": lax.rem(sec + 2, secs)}
         prev_sec = {"section": lax.rem(sec + secs - 2, secs)}
-        up = {"tensor": lax.rem(ten + 2, tens)}
-        down = {"tensor": lax.rem(ten + tens - 2, tens)}
 
         def remote(src, dst, where):
             return pltpu.make_async_remote_copy(
@@ -115,27 +113,26 @@
         def _():
             sw_ret.start()
 
-        start(*sw_hf, sw_hb)
-
-        @pl.when(sec < secs - 2)
-        def _():
-            sw_car.start()
-
-        def block(zz):
-            return lax.rem(zz + rings, rings) * 2 + core
-
-        def gather_copy(k, q, sign, where):
-            ref = cot.at[block(z - sign * (k - 1)), :, cols(q)]
+        def at_ring(k):
+            return lax.rem(z + k + rings, rings)
+
+        def on_ring(k):
+            return {"tensor": at_ring(k) * 2 + core}
+
+        def cot_copy(k, q, where):
+            ref = cot.at[at_ring(k) * 2 + core]
+            if q is not None:
+                ref = cot.at[at_ring(k) * 2 + core, :, cols(q)]
             return remote(ref, ref, where)
 
-        ag_up = {(k, q): gather_copy(k, q, 1, up) for k in range(1, far + 1) for q in (0, 1) if k < far or q == 0}
-        ag_dn = {(k, q): gather_copy(k, q, -1, down) for k in range(1, far + 1) for q in (0, 1) if k < far or q == 1}
-
-        def cross(zz, q=None):
-            ref = cot.at[block(zz)] if q is None else cot.at[block(zz), :, cols(q)]
-            return remote(ref, ref, sibling)
-
-        ag_x = [cross(z)]
+        first_q = {1: 0, -1: 1}
+        ag_own = {k: cot_copy(0, None, on_ring(k)) for k in (2, -2, 1, -1)}
+        ag_far = {}
+        ag_x = []
+
+        def cross(k):
+            ag_x.append(cot_copy(k, None, sibling))
+            start(ag_x[-1])
 
         def gather_first():
             @pl.when(sec < secs - 2)
@@ -146,25 +143,31 @@
             def _():
                 ld_cot.wait()
 
-            for q in (0, 1):
-                for ag in (ag_up, ag_dn):
-                    if (1, q) in ag:
-                        start(ag[1, q])
-            start(ag_x[0])
-
-        def gather_step(k):
-            for q in (0, 1):
-                for ag in (ag_up, ag_dn):
-                    if (k, q) in ag:
-                        ag[k, q].wait_recv()
-                        if (k + 1, q) in ag:
-                            start(ag[k + 1, q])
-            if k < far:
-                more = [cross(z - k), cross(z + k)]
-            else:
-                more = [cross(z - k, 0), cross(z + k, 1)]
-            start(*more)
-            ag_x.extend(more)
+            start(*ag_own.values())
+            cross(0)
+
+        def gather_second():
+            for d in (1, -1):
+                ag_own[2 * d].wait_recv()
+                ag_far[3 * d] = cot_copy(-2 * d, None, on_ring(d))
+                ag_far[4 * d] = cot_copy(-2 * d, first_q[d], on_ring(2 * d))
+                start(ag_far[3 * d], ag_far[4 * d])
+                cross(-2 * d)
+
+        def gather_near():
+            for d in (1, -1):
+                ag_own[d].wait_recv()
+                cross(-d)
+
+        def gather_last():
+            for d in (1, -1):
+                ag_far[3 * d].wait_recv()
+                cross(-3 * d)
+            for d in (1, -1):
+                ag_far[4 * d].wait_recv()
+            cross(4)
+            for copy in ag_x:
+                copy.wait_recv()
 
         def total_of(part, sib, slots, own_half):
             first = remote(part, sib, sibling)
@@ -202,16 +205,14 @@
 
         ld_a.wait()
         ld_b.wait()
-        ld_hb.wait()
         sw_a.wait_recv()
+        start(*sw_hf)
         mine, theirs = a_own[...].astype(f32), a_oth[...].astype(f32)
         first = half == 0
         a_all = jnp.concatenate(
             [jnp.where(first, mine, theirs), jnp.where(first, theirs, mine)], axis=0
         )
         s["at"][...] = a_all.T.astype(bf16)
-        s["lo"][...] = dot(a_all.astype(bf16), xb[half], 1, 1)
-        lo1()
 
         step_cols = min(256, width)
         step_rows = min(128, depth)
@@ -231,27 +232,25 @@
 
         ld_w.wait()
         n_merge = width // step_cols
-        lax.fori_loop(0, n_merge // 2, merge, 0)
+        lax.fori_loop(0, n_merge * 5 // 8, merge, 0)
         gather_first()
-        lo2()
-        lax.fori_loop(n_merge // 2, n_merge, merge, 0)
+        lax.fori_loop(n_merge * 5 // 8, n_merge, merge, 0)
         sq1()
-        gather_step(1)
+
+        ld_hb.wait()
+        s["lo"][...] = dot(a_all.astype(bf16), xb[half], 1, 1)
+        lo1()
         sq2()
-        low_own = lo3().astype(bf16)
-        s["low_own"][...] = low_own
-        sw_low = remote(s["low_own"], s["low_oth"], partner)
-        start(sw_low)
-        if far > 2:
-            gather_step(2)
 
         for copy in ld_hf:
             copy.wait()
         for copy in sw_hf:
             copy.wait_recv()
+        start(sw_hb)
+
         pcols = min(512, width)
 
-        def project(parity, keep):
+        def project(parity, keep, lo, hi):
             def body(i, carry):
                 cc = pl.ds(pl.multiple_of(i * pcols, pcols), pcols)
                 x = xf[parity].reshape(half_rows, depth)
@@ -259,22 +258,78 @@
                 keep[:, :, cc] = res.reshape(rings, 16, pcols).astype(keep.dtype)
                 return carry
 
-            lax.fori_loop(0, width // pcols, body, 0)
-
-        project(1 - core, s["p_send"])
-        sw_p = remote(s["p_send"], s["p_recv"], sibling)
-        start(sw_p)
-        for k in range(3 if far > 2 else 2, far):
-            gather_step(k)
-        project(core, s["pm"])
-        gather_step(far)
+            lax.fori_loop(lo // pcols, hi // pcols, body, 0)
+
+        sw_p = []
+        for q in (0, 1):
+            project(1 - core, s["p_send"], q * wide, (q + 1) * wide)
+            sw_p.append(remote(s["p_send"].at[:, :, cols(q)], s["p_recv"].at[:, :, cols(q)], sibling))
+            start(sw_p[q])
+        project(core, s["pm"], 0, width)
+        gather_second()
+        for copy in sw_p:
+            copy.wait_recv()
+
+        pm = s["pm"]
+
+        def term(k, q=None):
+            cc = slice(None) if q is None else cols(q)
+            return pm[at_ring(k), :, cc] + s["p_recv"][at_ring(k), :, cc].astype(f32)
+
+        rs = {}
+
+        def scatter(name, slot, val, q, where):
+            cc = slice(None) if q is None else cols(q)
+            s["rs_send"][slot, :, cc] = val.astype(bf16)
+            copy = remote(s["rs_send"].at[slot, :, cc], s["rs_recv"].at[slot, :, cc], where)
+            start(copy)
+            rs[name] = copy
+
+        def landed(name, slot, q=None):
+            cc = slice(None) if q is None else cols(q)
+            rs[name].wait_recv()
+            return s["rs_recv"][slot, :, cc].astype(f32)
+
+        ways = ((0, 1), (1, -1))
+        for i, d in ways:
+            scatter(("b", d), 2 + i, term(4, first_q[d]), first_q[d], on_ring(2 * d))
+            scatter(("a", d), i, term(3 * d), None, on_ring(d))
+        def scatter_second():
+            for i, d in ways:
+                mid = (term(2 * d, 0), term(2 * d, 1))
+                rs["a", d].wait_recv()
+                near = [mid[q] + s["rs_recv"][i, :, cols(q)].astype(f32) for q in (0, 1)]
+                near[first_q[d]] = near[first_q[d]] + landed(("b", d), 2 + i, first_q[d])
+                scatter(("c", d), 4 + i, jnp.concatenate(near, axis=1), None, on_ring(2 * d))
+
+        lo2()
+        gather_near()
+
+        @pl.when(sec < secs - 2)
+        def _():
+            sw_car.start()
 
         ld_mag.wait()
         norms = jnp.sqrt(sq3() + epsilon)
         s["norms"][...] = norms
         s["scale"][...] = mag[...] / norms
-        for copy in ag_x:
-            copy.wait_recv()
+
+        sw_hb.wait_recv()
+        rcols = min(512, width)
+        n_rec = width // rcols
+
+        def recompute(i, carry):
+            cc = pl.ds(pl.multiple_of(i * rcols, rcols), rcols)
+            s["rec"][:, cc] = dot(xb[...].reshape(2 * half_rows, depth), w[:, cc], 1, 0)
+            return carry
+
+        lax.fori_loop(0, n_rec, recompute, 0)
+        s["low_own"][...] = lo3().astype(bf16)
+        sw_low = remote(s["low_own"], s["low_oth"], partner)
+        start(sw_low)
+        gather_last()
+        for i, d in ways:
+            scatter(("d", d), 6 + i, term(d), None, on_ring(d))
 
         def rescale(i, carry):
             scot[i] = (cot[i].astype(f32) * s["scale"][...]).astype(bf16)
@@ -282,7 +337,14 @@
 
         lax.fori_loop(0, tens, rescale, 0)
 
-        hsplit = [(0, depth)] if depth < 896 else [(0, 512), (512, depth - 512)]
+        def magnitudes(i, carry):
+            cc = pl.ds(pl.multiple_of(i * step_cols, step_cols), step_cols)
+            got = cot[:, :, cc].reshape(2 * half_rows, step_cols).astype(f32)
+            part = jnp.sum((s["rec"][:, cc] * got).reshape(half_rows // 4, 8, step_cols), axis=0)
+            s["gmp"][:, cc] = jnp.sum(part, axis=0, keepdims=True)
+            return carry
+
+        hsplit = [(0, 512), (512, depth - 512)]
 
         def hidden(which, lo, size):
             rows = scot[pl.ds(which * blocks, blocks)].reshape(half_rows, width)
@@ -294,66 +356,20 @@
             copy = remote(s["hg_send"].at[:, pl.ds(lo, size)], s["hg_recv"].at[:, pl.ds(lo, size)], partner)
             start(copy)
             sw_hg.append(copy)
+            if lo == 0:
+                lax.fori_loop(0, n_merge, magnitudes, 0)
+                gm1()
 
         adapt = dot(b[...], scot[...].reshape(2 * half_rows, width), 1, 1)
         s["ad"][...] = adapt.reshape(2, 8, 2 * half_rows)
         sw_ad = remote(s["ad"].at[1 - half], s["ad_recv"], partner)
         start(sw_ad)
 
-        pm = s["pm"]
-        sw_p.wait_recv()
-
-        def merge_cores(i, carry):
-            pm[i] = pm[i] + s["p_recv"][i].astype(f32)
-            return carry
-
-        lax.fori_loop(0, rings, merge_cores, 0)
-        rs = {}
-
-        def scatter_step(k):
-            for q in (0, 1):
-                for name, sign, first_q, where in (("u", 1, 0, up), ("d", -1, 1, down)):
-                    if k == 1 and q != first_q:
-                        continue
-                    dest = lax.rem(z + sign * (far + 1 - k) + rings, rings)
-                    val = pm[dest, :, cols(q)]
-                    if (name, k - 1, q) in rs:
-                        rs[name, k - 1, q].wait_recv()
-                        val = val + s["rs_recv_" + name][k - 2, :, cols(q)].astype(f32)
-                    s["rs_send_" + name][k - 1, :, cols(q)] = val.astype(bf16)
-                    copy = remote(
-                        s["rs_send_" + name].at[k - 1, :, cols(q)],
-                        s["rs_recv_" + name].at[k - 1, :, cols(q)],
-                        where,
-                    )
-                    start(copy)
-                    rs[name, k, q] = copy
-
-        scatter_step(1)
-
-        for i, (lo, size) in enumerate(hsplit):
-            s["hg_own"][:, pl.ds(lo, size)] = hidden(half, lo, size)
-        scatter_step(2)
-
-        sw_hb.wait_recv()
-
-        def recompute(i, carry):
-            cc = pl.ds(pl.multiple_of(i * step_cols, step_cols), step_cols)
-            res = dot(xb[...].reshape(2 * half_rows, depth), w[:, cc], 1, 0)
-            got = cot[:, :, cc].reshape(2 * half_rows, step_cols).astype(f32)
-            part = jnp.sum((res * got).reshape(half_rows // 4, 8, step_cols), axis=0)
-            s["gmp"][:, cc] = jnp.sum(part, axis=0, keepdims=True)
-            return carry
-
-        n_rec = width // step_cols
-        lax.fori_loop(0, n_rec // 2, recompute, 0)
-        if far > 2:
-            scatter_step(3)
-        lax.fori_loop(n_rec // 2, n_rec, recompute, 0)
-        gm1()
-        for k in range(4 if far > 2 else 3, far + 1):
-            scatter_step(k)
+        scatter_second()
         gm2()
+
+        for lo_, size_ in hsplit:
+            s["hg_own"][:, pl.ds(lo_, size_)] = hidden(half, lo_, size_)
 
         sw_ad.wait_recv()
         own_ad = (s["ad"][half] + s["ad_recv"][...]).astype(bf16)
@@ -369,28 +385,25 @@
         out_gb = local(s["gb"], gb_out.at[0])
         out_gb.start()
 
-        @pl.when(sec < 2)
-        def _():
-            ld_infl.wait()
-
-        @pl.when(sec >= 2)
-        def _():
-            sw_car.wait_recv()
-
-        for q in (0, 1):
-            val = pm[z, :, cols(q)]
-            for name in "ud":
-                if (name, far, q) in rs:
-                    rs[name, far, q].wait_recv()
-                    val = val + s["rs_recv_" + name][far - 1, :, cols(q)].astype(f32)
-            val = infl[:, cols(q)].astype(f32) + val * s["scale"][:, cols(q)]
-            s["so"][:, cols(q)] = val.astype(bf16)
-        out_so = local(s["so"], so_out.at[0])
-        out_so.start()
-
         s["gm"][...] = gm3() / s["norms"][...]
         out_gm = local(s["gm"], gm_out)
         out_gm.start()
+
+        @pl.when(sec < 2)
+        def _():
+            ld_infl.wait()
+
+        @pl.when(sec >= 2)
+        def _():
+            sw_car.wait_recv()
+
+        val = term(0)
+        for i, d in ways:
+            val = val + landed(("d", d), 6 + i) + landed(("c", d), 4 + i)
+        val = infl[...].astype(f32) + val * s["scale"][...]
+        s["so"][...] = val.astype(bf16)
+        out_so = local(s["so"], so_out.at[0])
+        out_so.start()
 
         for copy in sw_hg:
             copy.wait_recv()
@@ -415,12 +428,24 @@
     return kernel
 
 
+def hand_over(*refs):
+    given, results, held, sems = refs[:5], refs[5:10], refs[10:15], refs[15]
+    into = [pltpu.make_async_copy(given[i], held[i], sems.at[i]) for i in range(5)]
+    out = [pltpu.make_async_copy(held[i], results[i], sems.at[5 + i]) for i in range(5)]
+    for copy in into:
+        copy.start()
+    for i in range(5):
+        into[i].wait()
+        out[i].start()
+    for copy in out:
+        copy.wait()
+
+
 def local(secs, tens, *args):
     (frozen, adapter_a, adapter_b, magnitude, hidden_fwd, carried, embedded, hidden_bwd, returned, head) = args
     depth, width = frozen.shape[1:]
     half_rows = hidden_fwd.shape[1]
     rings = tens // 2
-    far = rings // 2
     n_sems = 320
     shapes = {
         "w": pltpu.VMEM((depth, width), bf16),
@@ -450,10 +475,9 @@
         "p_send": pltpu.VMEM((rings, 16, width), bf16),
         "p_recv": pltpu.VMEM((rings, 16, width), bf16),
         "pm": pltpu.VMEM((rings, 16, width), f32),
-        "rs_send_u": pltpu.VMEM((far, 16, width), bf16),
-        "rs_recv_u": pltpu.VMEM((far, 16, width), bf16),
-        "rs_send_d": pltpu.VMEM((far, 16, width), bf16),
-        "rs_recv_d": pltpu.VMEM((far, 16, width), bf16),
+        "rs_send": pltpu.VMEM((8, 16, width), bf16),
+        "rs_recv": pltpu.VMEM((8, 16, width), bf16),
+        "rec": pltpu.VMEM((2 * half_rows, width), f32),
         "hg_send": pltpu.VMEM((half_rows, depth), bf16),
         "hg_recv": pltpu.VMEM((half_rows, depth), bf16),
         "hg_own": pltpu.VMEM((half_rows, depth), f32),
@@ -467,7 +491,7 @@
         "sems": pltpu.SemaphoreType.DMA((n_sems,)),
     }
     anywhere = pl.BlockSpec(memory_space=pl.ANY)
-    return pl.pallas_call(
+    results = pl.pallas_call(
         make_kernel(secs, tens, list(shapes), n_sems),
         out_shape=(
             jax.ShapeDtypeStruct((1, 16, width), bf16),
@@ -480,7 +504,7 @@
         out_specs=(anywhere,) * 5,
         scratch_shapes=list(shapes.values()),
         compiler_params=pltpu.CompilerParams(
-            collective_id=0, has_side_effects=True, vmem_limit_bytes=48 * 1024 * 1024
+            collective_id=0, has_side_effects=True, vmem_limit_bytes=63 * 1024 * 1024
         ),
     )(
         frozen,
@@ -494,6 +518,14 @@
         returned,
         head,
     )
+    return pl.pallas_call(
+        hand_over,
+        out_shape=[jax.ShapeDtypeStruct(r.shape, r.dtype) for r in results],
+        in_specs=[anywhere] * 5,
+        out_specs=[anywhere] * 5,
+        scratch_shapes=[pltpu.VMEM(r.shape, r.dtype) for r in results] + [pltpu.SemaphoreType.DMA((10,))],
+        compiler_params=pltpu.CompilerParams(vmem_limit_bytes=63 * 1024 * 1024),
+    )(*results)
 
 
 def solution(mesh):

time: 71.1 us -> 53.3 us (0.75)
  local copies, waits for them, and re-layouts: 12.8 us -> 0 us
  Pallas kernels: 57.1 us -> 52.6 us
    unnamed x25 -> x0, local copies, waits for them, and re-layouts: 12.8 us -> none
    pallas_call x1, Pallas kernels: 57.1 us -> 50.7 us  [local(): pl.pallas_call(make_kernel(secs, tens, list(shapes), n_sems), out_shape=(...]
    pallas_call x0 -> x1, Pallas kernels: none -> 1.85 us  [local(): pl.pallas_call(hand_over, out_shape=[jax.ShapeDtypeStruct(r.shape, r.dtyp...]
where the time goes in v2:
time: 53.3 us; the launch traced here: 53.2 us
  Pallas kernels  52.6 us (99%)
  between operations  0.64 us (1%)
    pallas_call x1, Pallas kernels, local(): pl.pallas_call(make_kernel(secs, tens, list(shapes), n_sems), out_shape=(...  50.7 us
    pallas_call x1, Pallas kernels, local(): pl.pallas_call(hand_over, out_shape=[jax.ShapeDtypeStruct(r.shape, r.dtyp...  1.85 us

profile of v2, /device:TPU:1, one launch (start us, length us, event | category | flops | bytes accessed | tf_op | source)
XLA Modules:
  0.0 53.2 jit_solution(13830929529343190204)
XLA Ops:
  0.6 50.7 %shard_map.137 = (bf16[1,16,2048]{2,1,0:T(8,128)(2,1)}, f32[1,2048]{1,0:T(1,128)}, f32[1,8,896]{2,1,0:T(8,128)}, f32[1,16,2048]{2,1,0:T(8,128)}, bf16[1,128,896]{2,1,0:T(8,128)(2,1)}) custom-call(bf16[1,896,2048]{2,1,0:T(8,128)(2,1)} %refs_0_.1, bf16[1,8,896]{2,1,0:T(8,128)(2,1)} %refs_1_.1, bf16[1,16,2048]{2,1,0:T(8,128)(2,1)} %refs_2_.1, ...), custom_call_target="tpu_custom_call" | custom-call | tf_op jit(solution)/shard_map/pallas_call | solution.py:494
  51.4 1.9 %shard_map.138 = (bf16[1,16,2048]{2,1,0:T(8,128)(2,1)}, f32[1,2048]{1,0:T(1,128)}, f32[1,8,896]{2,1,0:T(8,128)}, f32[1,16,2048]{2,1,0:T(8,128)}, bf16[1,128,896]{2,1,0:T(8,128)(2,1)}) custom-call(bf16[1,16,2048]{2,1,0:T(8,128)(2,1)} %get-tuple-element.10.refs_0_, f32[1,2048]{1,0:T(1,128)} %get-tuple-element.11.refs_1_, ...), custom_call_target="tpu_custom_call" | custom-call | tf_op jit(solution)/shard_map/pallas_call | solution.py:521

commit v3 on v2

--- a/solution.py
+++ b/solution.py
@@ -265,8 +265,8 @@
             project(1 - core, s["p_send"], q * wide, (q + 1) * wide)
             sw_p.append(remote(s["p_send"].at[:, :, cols(q)], s["p_recv"].at[:, :, cols(q)], sibling))
             start(sw_p[q])
+        gather_second()
         project(core, s["pm"], 0, width)
-        gather_second()
         for copy in sw_p:
             copy.wait_recv()
 
@@ -302,12 +302,7 @@
                 near[first_q[d]] = near[first_q[d]] + landed(("b", d), 2 + i, first_q[d])
                 scatter(("c", d), 4 + i, jnp.concatenate(near, axis=1), None, on_ring(2 * d))
 
-        lo2()
         gather_near()
-
-        @pl.when(sec < secs - 2)
-        def _():
-            sw_car.start()
 
         ld_mag.wait()
         norms = jnp.sqrt(sq3() + epsilon)
@@ -324,10 +319,8 @@
             return carry
 
         lax.fori_loop(0, n_rec, recompute, 0)
-        s["low_own"][...] = lo3().astype(bf16)
-        sw_low = remote(s["low_own"], s["low_oth"], partner)
-        start(sw_low)
         gather_last()
+        lo2()
         for i, d in ways:
             scatter(("d", d), 6 + i, term(d), None, on_ring(d))
 
@@ -343,6 +336,9 @@
             part = jnp.sum((s["rec"][:, cc] * got).reshape(half_rows // 4, 8, step_cols), axis=0)
             s["gmp"][:, cc] = jnp.sum(part, axis=0, keepdims=True)
             return carry
+
+        lax.fori_loop(0, n_merge, magnitudes, 0)
+        gm1()
 
         hsplit = [(0, 512), (512, depth - 512)]
 
@@ -357,8 +353,11 @@
             start(copy)
             sw_hg.append(copy)
             if lo == 0:
-                lax.fori_loop(0, n_merge, magnitudes, 0)
-                gm1()
+                gm2()
+
+        @pl.when(sec < secs - 2)
+        def _():
+            sw_car.start()
 
         adapt = dot(b[...], scot[...].reshape(2 * half_rows, width), 1, 1)
         s["ad"][...] = adapt.reshape(2, 8, 2 * half_rows)
@@ -366,11 +365,13 @@
         start(sw_ad)
 
         scatter_second()
-        gm2()
 
         for lo_, size_ in hsplit:
             s["hg_own"][:, pl.ds(lo_, size_)] = hidden(half, lo_, size_)
 
+        s["low_own"][...] = lo3().astype(bf16)
+        sw_low = remote(s["low_own"], s["low_oth"], partner)
+        start(sw_low)
         sw_ad.wait_recv()
         own_ad = (s["ad"][half] + s["ad_recv"][...]).astype(bf16)
         s["ga"][...] = dot(own_ad, xb[...].reshape(2 * half_rows, depth), 1, 0)

time: 53.3 us -> 49.6 us (0.931)
  the two profiles are of different devices: /device:TPU:1 before, /device:TPU:7 now
where the time goes in v3:
time: 49.6 us; the launch traced here: 49.5 us
  Pallas kernels  48.8 us (98%)
  between operations  0.64 us (1%)
    pallas_call x1, Pallas kernels, local(): pl.pallas_call(make_kernel(secs, tens, list(shapes), n_sems), out_shape=(...  47 us
    pallas_call x1, Pallas kernels, local(): pl.pallas_call(hand_over, out_shape=[jax.ShapeDtypeStruct(r.shape, r.dtyp...  1.85 us

profile of v3, /device:TPU:7, one launch (start us, length us, event | category | flops | bytes accessed | tf_op | source)
XLA Modules:
  0.0 49.5 jit_solution(5433603097456534742)
XLA Ops:
  0.6 47.0 %shard_map.137 = (bf16[1,16,2048]{2,1,0:T(8,128)(2,1)}, f32[1,2048]{1,0:T(1,128)}, f32[1,8,896]{2,1,0:T(8,128)}, f32[1,16,2048]{2,1,0:T(8,128)}, bf16[1,128,896]{2,1,0:T(8,128)(2,1)}) custom-call(bf16[1,896,2048]{2,1,0:T(8,128)(2,1)} %refs_0_.1, bf16[1,8,896]{2,1,0:T(8,128)(2,1)} %refs_1_.1, bf16[1,16,2048]{2,1,0:T(8,128)(2,1)} %refs_2_.1, ...), custom_call_target="tpu_custom_call" | custom-call | tf_op jit(solution)/shard_map/pallas_call | solution.py:495
  47.6 1.9 %shard_map.138 = (bf16[1,16,2048]{2,1,0:T(8,128)(2,1)}, f32[1,2048]{1,0:T(1,128)}, f32[1,8,896]{2,1,0:T(8,128)}, f32[1,16,2048]{2,1,0:T(8,128)}, bf16[1,128,896]{2,1,0:T(8,128)(2,1)}) custom-call(bf16[1,16,2048]{2,1,0:T(8,128)(2,1)} %get-tuple-element.10.refs_0_, f32[1,2048]{1,0:T(1,128)} %get-tuple-element.11.refs_1_, ...), custom_call_target="tpu_custom_call" | custom-call | tf_op jit(solution)/shard_map/pallas_call | solution.py:522

commit v4 on v3

--- a/solution.py
+++ b/solution.py
@@ -100,7 +100,7 @@
         pl.semaphore_wait(barrier, len(everyone))
 
         sw_a = remote(a_in.at[0], a_oth, partner)
-        sw_ret = remote(ret_in.at[0], cot.at[ten], prev_sec)
+        sw_ret = [remote(ret_in.at[0, :, cols(q)], cot.at[ten, :, cols(q)], prev_sec) for q in (0, 1)]
         sw_hf = [
             remote(hf_in.at[:, p], xf.at[p, pl.ds(half * (blocks // 2), blocks // 2)], partner)
             for p in (0, 1)
@@ -111,7 +111,8 @@
 
         @pl.when(sec >= 2)
         def _():
-            sw_ret.start()
+            for copy in sw_ret:
+                copy.start()
 
         def at_ring(k):
             return lax.rem(z + k + rings, rings)
@@ -126,7 +127,7 @@
             return remote(ref, ref, where)
 
         first_q = {1: 0, -1: 1}
-        ag_own = {k: cot_copy(0, None, on_ring(k)) for k in (2, -2, 1, -1)}
+        ag_own = {(k, q): cot_copy(0, q, on_ring(k)) for q in (0, 1) for k in (2, -2, 1, -1)}
         ag_far = {}
         ag_x = []
 
@@ -135,33 +136,40 @@
             start(ag_x[-1])
 
         def gather_first():
-            @pl.when(sec < secs - 2)
-            def _():
-                sw_ret.wait_recv()
-
             @pl.when(sec >= secs - 2)
             def _():
                 ld_cot.wait()
 
-            start(*ag_own.values())
+            for q in (0, 1):
+
+                @pl.when(sec < secs - 2)
+                def _():
+                    sw_ret[q].wait_recv()
+
+                start(*[ag_own[k, q] for k in (2, -2, 1, -1)])
             cross(0)
 
-        def gather_second():
+        def gather_second(q):
             for d in (1, -1):
-                ag_own[2 * d].wait_recv()
-                ag_far[3 * d] = cot_copy(-2 * d, None, on_ring(d))
-                ag_far[4 * d] = cot_copy(-2 * d, first_q[d], on_ring(2 * d))
-                start(ag_far[3 * d], ag_far[4 * d])
-                cross(-2 * d)
+                ag_own[2 * d, q].wait_recv()
+                ag_far[3 * d, q] = cot_copy(-2 * d, q, on_ring(d))
+                start(ag_far[3 * d, q])
+                if q == first_q[d]:
+                    ag_far[4 * d] = cot_copy(-2 * d, q, on_ring(2 * d))
+                    start(ag_far[4 * d])
+                if q == 1:
+                    cross(-2 * d)
 
         def gather_near():
             for d in (1, -1):
-                ag_own[d].wait_recv()
+                for q in (0, 1):
+                    ag_own[d, q].wait_recv()
                 cross(-d)
 
         def gather_last():
             for d in (1, -1):
-                ag_far[3 * d].wait_recv()
+                for q in (0, 1):
+                    ag_far[3 * d, q].wait_recv()
                 cross(-3 * d)
             for d in (1, -1):
                 ag_far[4 * d].wait_recv()
@@ -260,12 +268,13 @@
 
             lax.fori_loop(lo // pcols, hi // pcols, body, 0)
 
+        gather_second(0)
         sw_p = []
         for q in (0, 1):
             project(1 - core, s["p_send"], q * wide, (q + 1) * wide)
             sw_p.append(remote(s["p_send"].at[:, :, cols(q)], s["p_recv"].at[:, :, cols(q)], sibling))
             start(sw_p[q])
-        gather_second()
+        gather_second(1)
         project(core, s["pm"], 0, width)
         for copy in sw_p:
             copy.wait_recv()
@@ -354,6 +363,7 @@
             sw_hg.append(copy)
             if lo == 0:
                 gm2()
+                scatter_second()
 
         @pl.when(sec < secs - 2)
         def _():
@@ -364,7 +374,6 @@
         sw_ad = remote(s["ad"].at[1 - half], s["ad_recv"], partner)
         start(sw_ad)
 
-        scatter_second()
 
         for lo_, size_ in hsplit:
             s["hg_own"][:, pl.ds(lo_, size_)] = hidden(half, lo_, size_)
@@ -374,21 +383,15 @@
         start(sw_low)
         sw_ad.wait_recv()
         own_ad = (s["ad"][half] + s["ad_recv"][...]).astype(bf16)
-        s["ga"][...] = dot(own_ad, xb[...].reshape(2 * half_rows, depth), 1, 0)
-        out_ga = local(s["ga"], ga_out.at[0])
-        out_ga.start()
+        ga_out[0] = dot(own_ad, xb[...].reshape(2 * half_rows, depth), 1, 0)
         sw_low.wait_recv()
-        s["gb"][...] = dot(
+        gb_out[0] = dot(
             s["low_own"][...], scot[pl.ds(half * blocks, blocks)].reshape(half_rows, width), 1, 0
         ) + dot(
             s["low_oth"][...], scot[pl.ds((1 - half) * blocks, blocks)].reshape(half_rows, width), 1, 0
         )
-        out_gb = local(s["gb"], gb_out.at[0])
-        out_gb.start()
-
-        s["gm"][...] = gm3() / s["norms"][...]
-        out_gm = local(s["gm"], gm_out)
-        out_gm.start()
+
+        gm_out[...] = gm3() / s["norms"][...]
 
         @pl.when(sec < 2)
         def _():
@@ -402,43 +405,34 @@
         for i, d in ways:
             val = val + landed(("d", d), 6 + i) + landed(("c", d), 4 + i)
         val = infl[...].astype(f32) + val * s["scale"][...]
-        s["so"][...] = val.astype(bf16)
-        out_so = local(s["so"], so_out.at[0])
-        out_so.start()
+        so_out[0] = val.astype(bf16)
 
         for copy in sw_hg:
             copy.wait_recv()
-        s["hg"][...] = (s["hg_own"][...] + s["hg_recv"][...].astype(f32)).astype(bf16)
-        out_hg = local(s["hg"], hg_out.at[0])
-        out_hg.start()
+        hg_out[0] = (s["hg_own"][...] + s["hg_recv"][...].astype(f32)).astype(bf16)
 
         for copy in sent:
             copy.wait_send()
 
         @pl.when(sec >= 2)
         def _():
-            sw_ret.wait_send()
+            for copy in sw_ret:
+                copy.wait_send()
 
         @pl.when(sec < secs - 2)
         def _():
             sw_car.wait_send()
 
-        for copy in (out_ga, out_gb, out_so, out_gm, out_hg):
-            copy.wait()
 
     return kernel
 
 
 def hand_over(*refs):
-    given, results, held, sems = refs[:5], refs[5:10], refs[10:15], refs[15]
-    into = [pltpu.make_async_copy(given[i], held[i], sems.at[i]) for i in range(5)]
-    out = [pltpu.make_async_copy(held[i], results[i], sems.at[5 + i]) for i in range(5)]
-    for copy in into:
+    sems = refs[10]
+    copies = [pltpu.make_async_copy(refs[i], refs[5 + i], sems.at[i]) for i in range(5)]
+    for copy in copies:
         copy.start()
-    for i in range(5):
-        into[i].wait()
-        out[i].start()
-    for copy in out:
+    for copy in copies:
         copy.wait()
 
 
@@ -484,28 +478,23 @@
         "hg_own": pltpu.VMEM((half_rows, depth), f32),
         "ad": pltpu.VMEM((2, 8, 2 * half_rows), f32),
         "ad_recv": pltpu.VMEM((8, 2 * half_rows), f32),
-        "so": pltpu.VMEM((16, width), bf16),
-        "gm": pltpu.VMEM((1, width), f32),
-        "ga": pltpu.VMEM((8, depth), f32),
-        "gb": pltpu.VMEM((16, width), f32),
-        "hg": pltpu.VMEM((half_rows, depth), bf16),
         "sems": pltpu.SemaphoreType.DMA((n_sems,)),
     }
     anywhere = pl.BlockSpec(memory_space=pl.ANY)
     results = pl.pallas_call(
         make_kernel(secs, tens, list(shapes), n_sems),
         out_shape=(
-            jax.ShapeDtypeStruct((1, 16, width), bf16),
-            jax.ShapeDtypeStruct((1, width), f32),
-            jax.ShapeDtypeStruct((1, 8, depth), f32),
-            jax.ShapeDtypeStruct((1, 16, width), f32),
-            jax.ShapeDtypeStruct((1, half_rows, depth), bf16),
+            pltpu.VMEM((1, 16, width), bf16),
+            pltpu.VMEM((1, width), f32),
+            pltpu.VMEM((1, 8, depth), f32),
+            pltpu.VMEM((1, 16, width), f32),
+            pltpu.VMEM((1, half_rows, depth), bf16),
         ),
         in_specs=[anywhere] * 10,
-        out_specs=(anywhere,) * 5,
+        out_specs=(pl.BlockSpec(memory_space=pltpu.VMEM),) * 5,
         scratch_shapes=list(shapes.values()),
         compiler_params=pltpu.CompilerParams(
-            collective_id=0, has_side_effects=True, vmem_limit_bytes=63 * 1024 * 1024
+            collective_id=0, has_side_effects=True, vmem_limit_bytes=62 * 1024 * 1024
         ),
     )(
         frozen,
@@ -522,10 +511,10 @@
     return pl.pallas_call(
         hand_over,
         out_shape=[jax.ShapeDtypeStruct(r.shape, r.dtype) for r in results],
-        in_specs=[anywhere] * 5,
+        in_specs=[pl.BlockSpec(memory_space=pltpu.VMEM)] * 5,
         out_specs=[anywhere] * 5,
-        scratch_shapes=[pltpu.VMEM(r.shape, r.dtype) for r in results] + [pltpu.SemaphoreType.DMA((10,))],
-        compiler_params=pltpu.CompilerParams(vmem_limit_bytes=63 * 1024 * 1024),
+        scratch_shapes=[pltpu.SemaphoreType.DMA((5,))],
+        compiler_params=pltpu.CompilerParams(vmem_limit_bytes=4 * 1024 * 1024),
     )(*results)
 
 

time: 49.6 us -> 48 us (0.968)
  Pallas kernels: 48.8 us -> 47.2 us
    pallas_call x1, Pallas kernels: 1.85 us -> 0.81 us  [local(): pl.pallas_call(hand_over, out_shape=[jax.ShapeDtypeStruct(r.shape, r.dtyp...]
    pallas_call x1, Pallas kernels: 47 us -> 46.4 us  [local(): pl.pallas_call(make_kernel(secs, tens, list(shapes), n_sems), out_shape=(...]
where the time goes in v4:
time: 48 us; the launch traced here: 47.9 us
  Pallas kernels  47.2 us (98%)
  between operations  0.64 us (1%)
    pallas_call x1, Pallas kernels, local(): pl.pallas_call(make_kernel(secs, tens, list(shapes), n_sems), out_shape=(...  46.4 us

profile of v4, /device:TPU:7, one launch (start us, length us, event | category | flops | bytes accessed | tf_op | source)
XLA Modules:
  0.0 47.9 jit_solution(9528728706242399373)
XLA Ops:
  0.6 46.4 %shard_map.137 = (bf16[1,16,2048]{2,1,0:T(8,128)(2,1)S(1)}, f32[1,2048]{1,0:T(1,128)S(1)}, f32[1,8,896]{2,1,0:T(8,128)S(1)}, f32[1,16,2048]{2,1,0:T(8,128)S(1)}, bf16[1,128,896]{2,1,0:T(8,128)(2,1)S(1)}) custom-call(bf16[1,896,2048]{2,1,0:T(8,128)(2,1)} %refs_0_.1, bf16[1,8,896]{2,1,0:T(8,128)(2,1)} %refs_1_.1, bf16[1,16,2048]{2,1,0:T(8,128)(2,1)} %refs_2_.1, ...), custom_call_target="tpu_custom_call" | custom-call | tf_op jit(solution)/shard_map/pallas_call | solution.py:484
  47.1 0.8 %shard_map.138 = (bf16[1,16,2048]{2,1,0:T(8,128)(2,1)}, f32[1,2048]{1,0:T(1,128)}, f32[1,8,896]{2,1,0:T(8,128)}, f32[1,16,2048]{2,1,0:T(8,128)}, bf16[1,128,896]{2,1,0:T(8,128)(2,1)}) custom-call(bf16[1,16,2048]{2,1,0:T(8,128)(2,1)S(1)} %get-tuple-element.10.refs_0_, f32[1,2048]{1,0:T(1,128)S(1)} %get-tuple-element.11.refs_1_, ...), custom_call_target="tpu_custom_call" | custom-call | tf_op jit(solution)/shard_map/pallas_call | solution.py:511
